TPU v7x, 32 devices: a whole 2x2x4 slice. The times are simulated.
32 devices in a mesh: mix: 2 (over x), seq: 16 (over z, y, core).
Axes of the slice: x: 2, y: 2, z: 4, core: 2. Of those that a mesh axis runs over, the one named last changes fastest.
Arguments:
- frames: bfloat16 [4096, 1024], P(('mix', 'seq')), parts along dimension 0, may hold values from -18 to 18
- segment_ids: int32 [4096], P(('mix', 'seq')), parts along dimension 0, may hold values from 0 to 2, never falling along the last dimension, each value on 1 to 1500 neighbouring positions
- out_grad: bfloat16 [4096, 1024], P(('mix', 'seq')), parts along dimension 0, may hold values from -6 to 6
- ln_gain: float32 [2048], P(('mix', 'seq')), parts along dimension 0, may hold values from 0.5 to 2
- w_in: bfloat16 [2048, 2048], P(('mix', 'seq')), parts along dimension 0, may hold values from -0.1875 to 0.1875
- dw_kernel: float32 [62, 1024], P('mix', 'seq'), parts along dimension 0, may hold values from -1 to 1
- bn_gain: float32 [2048], P(('mix', 'seq')), parts along dimension 0, may hold values from 0.5 to 2
- bn_bias: float32 [2048], P(('mix', 'seq')), parts along dimension 0, may hold values from -3 to 3
- w_out: bfloat16 [2048, 1024], P(('mix', 'seq')), parts along dimension 0, may hold values from -0.1875 to 0.1875
Outputs:
- outputs: bfloat16 [4096, 1024], P(('mix', 'seq')), parts along dimension 0
- grad_frames: bfloat16 [4096, 1024], P(('mix', 'seq')), parts along dimension 0
- grad_w_in: float32 [2048, 2048], P(('mix', 'seq')), parts along dimension 0
- grad_w_out: float32 [2048, 1024], P(('mix', 'seq')), parts along dimension 0
- grad_kernel: float32 [62, 1024], P('mix', 'seq'), parts along dimension 0
- grad_ln_gain: float32 [2048], P(('mix', 'seq')), parts along dimension 0
- grad_bn_gain: float32 [2048], P(('mix', 'seq')), parts along dimension 0
- grad_bn_bias: float32 [2048], P(('mix', 'seq')), parts along dimension 0
There are 2 independent parts, one for each index of `mix`. A program takes and returns all parts, laid end to end along the dimension named above; each array names one. Nothing has to cross between parts.
Inputs may be any that keep to these rules, and one draw needn't show every extreme that they name: `segment_ids`: ids never fall along the stream; every utterance number is used, by 1 to 1500 consecutive frames, one utterance exactly 1500.
All inputs are finite; a program needn't handle non-finite values.
Results may differ from a plain program's by a relative error of at most 0.012.
The roundings to bfloat16 on the way count: a program that leaves them out, or rounds other values in their place, can miss the bound.
Values may be sent and summed in bfloat16 or wider, within the bound.
A program may use at most 128 MiB of HBM per device.

v0:
```python
import math

import jax
import jax.numpy as jnp
from jax import lax
from jax.sharding import PartitionSpec as P

EPSILON = 1e-05


def with_halo(cells, sides, width):
    for axis, dim in sides:
        count = lax.axis_size(axis)
        ends = count - 1
        head = lax.slice_in_dim(cells, 0, width, axis=dim)
        tail = lax.slice_in_dim(cells, cells.shape[dim] - width, cells.shape[dim], axis=dim)
        cells = jnp.concatenate(
            [
                lax.ppermute(tail, axis, [(i, (i + 1) % count) for i in range(ends)]),
                cells,
                lax.ppermute(head, axis, [((i + 1) % count, i) for i in range(ends)]),
            ],
            axis=dim,
        )
    return cells


def local(frames, segment_ids, out_grad, ln_gain, w_in, dw_kernel, bn_gain, bn_bias, w_out):
    frame_count = frames.shape[0]
    width = frames.shape[1]
    taps = dw_kernel.shape[0]
    margin = taps // 2
    devices = lax.axis_size("seq")
    stream = frame_count * devices
    grad_scale = 1.0 / math.sqrt(stream)
    share = width // devices
    gains, kernel, bn_scale, bn_shift = (
        lax.all_gather(ln_gain, "seq", axis=0, tiled=True),
        lax.all_gather(dw_kernel, "seq", axis=1, tiled=True),
        lax.all_gather(bn_gain, "seq", axis=0, tiled=True),
        lax.all_gather(bn_bias, "seq", axis=0, tiled=True),
    )
    own_ids = segment_ids + 1
    padded_ids = with_halo(own_ids, (("seq", 0),), margin)
    masks = [
        (padded_ids[tap_index : tap_index + frame_count] == own_ids).astype(jnp.float32)[:, None]
        for tap_index in range(taps)
    ]
    frames_float = frames.astype(jnp.float32)
    mean_ln = jnp.mean(frames_float, axis=1, keepdims=True)
    centred = frames_float - mean_ln
    rstd_ln = lax.rsqrt(jnp.mean(centred * centred, axis=1, keepdims=True) + EPSILON)
    ln_hat = centred * rstd_ln
    ln_x = (ln_hat * gains).astype(jnp.bfloat16)
    columns = ln_x
    hidden = jnp.dot(
        columns, lax.all_gather(w_in, "seq", axis=0, tiled=True), preferred_element_type=jnp.float32
    )
    left_half = hidden[:, :width]
    right_gate = jax.nn.sigmoid(hidden[:, width:])
    glu = (left_half * right_gate).astype(jnp.bfloat16)
    padded_glu = with_halo(glu, (("seq", 0),), margin)
    conv_out = jnp.zeros((frame_count, width), jnp.float32)
    for tap_index in range(taps):
        conv_out = (
            conv_out
            + kernel[tap_index]
            * padded_glu[tap_index : tap_index + frame_count].astype(jnp.float32)
            * masks[tap_index]
        )
    plain_sums, square_sums = lax.psum(
        (jnp.sum(conv_out, axis=0), jnp.sum(conv_out * conv_out, axis=0)), "seq"
    )
    bn_mean = plain_sums / stream
    bn_var = square_sums / stream - bn_mean * bn_mean
    bn_rstd = lax.rsqrt(bn_var + EPSILON)
    bn_hat = (conv_out - bn_mean) * bn_rstd
    zed = bn_hat * bn_scale + bn_shift
    zed_gate = jax.nn.sigmoid(zed)
    activation = (zed * zed_gate).astype(jnp.bfloat16)
    columns = activation
    projected = jnp.dot(
        columns,
        lax.all_gather(w_out, "seq", axis=0, tiled=True),
        preferred_element_type=jnp.float32,
    )
    outputs = (frames_float + projected).astype(jnp.bfloat16)
    grad_w_out = lax.psum_scatter(
        jnp.einsum("fa,fb->ab", activation, out_grad, preferred_element_type=jnp.float32)
        * grad_scale,
        "seq",
        scatter_dimension=0,
        tiled=True,
    )
    grad_act = jnp.einsum(
        "fe,ne->fn",
        out_grad,
        lax.all_gather(w_out, "seq", axis=0, tiled=True),
        preferred_element_type=jnp.float32,
    )
    grad_zed = grad_act * zed_gate * (1.0 + zed * (1.0 - zed_gate))
    bias_total, gain_total = lax.psum(
        (jnp.sum(grad_zed, axis=0), jnp.sum(grad_zed * bn_hat, axis=0)), "seq"
    )
    grad_conv = bn_scale * bn_rstd * (grad_zed - bias_total / stream - bn_hat * gain_total / stream)
    first_channel = lax.axis_index("seq") * share
    grad_bn_bias = lax.dynamic_slice_in_dim(bias_total, first_channel, share, 0) * grad_scale
    grad_bn_gain = lax.dynamic_slice_in_dim(gain_total, first_channel, share, 0) * grad_scale
    kernel_rows = [
        jnp.sum(
            grad_conv
            * padded_glu[tap_index : tap_index + frame_count].astype(jnp.float32)
            * masks[tap_index],
            axis=0,
        )
        for tap_index in range(taps)
    ]
    kernel_term = jnp.stack(kernel_rows) * grad_scale
    padded_conv = with_halo(grad_conv, (("seq", 0),), margin)
    grad_glu = jnp.zeros((frame_count, width), jnp.float32)
    for tap_index in range(taps):
        mirror = 2 * margin - tap_index
        grad_glu = (
            grad_glu
            + kernel[tap_index] * padded_conv[mirror : mirror + frame_count] * masks[mirror]
        )
    grad_hidden = jnp.concatenate(
        [grad_glu * right_gate, grad_glu * left_half * right_gate * (1.0 - right_gate)], axis=1
    ).astype(jnp.bfloat16)
    grad_ln = jnp.einsum(
        "fe,ne->fn",
        grad_hidden,
        lax.all_gather(w_in, "seq", axis=0, tiled=True),
        preferred_element_type=jnp.float32,
    )
    in_term = (
        jnp.einsum("fa,fb->ab", ln_x, grad_hidden, preferred_element_type=jnp.float32) * grad_scale
    )
    gain_term = jnp.sum(grad_ln * ln_hat, axis=0) * grad_scale
    grad_w_in, grad_kernel, grad_ln_gain = (
        lax.psum_scatter(in_term, "seq", scatter_dimension=0, tiled=True),
        lax.psum_scatter(kernel_term, "seq", scatter_dimension=1, tiled=True),
        lax.psum_scatter(gain_term, "seq", scatter_dimension=0, tiled=True),
    )
    grad_hat = grad_ln * gains
    grad_input = rstd_ln * (
        grad_hat
        - jnp.mean(grad_hat, axis=1, keepdims=True)
        - ln_hat * jnp.mean(grad_hat * ln_hat, axis=1, keepdims=True)
    )
    grad_frames = (out_grad.astype(jnp.float32) + grad_input).astype(jnp.bfloat16)
    return (
        outputs,
        grad_frames,
        grad_w_in,
        grad_w_out,
        grad_kernel,
        grad_ln_gain,
        grad_bn_gain,
        grad_bn_bias,
    )


def solution(mesh):
    return jax.shard_map(
        local,
        mesh=mesh,
        in_specs=(
            P(("mix", "seq"), None),
            P(("mix", "seq")),
            P(("mix", "seq"), None),
            P(("mix", "seq")),
            P(("mix", "seq"), None),
            P("mix", "seq"),
            P(("mix", "seq")),
            P(("mix", "seq")),
            P(("mix", "seq"), None),
        ),
        out_specs=(
            P(("mix", "seq"), None),
            P(("mix", "seq"), None),
            P(("mix", "seq"), None),
            P(("mix", "seq"), None),
            P("mix", "seq"),
            P(("mix", "seq")),
            P(("mix", "seq")),
            P(("mix", "seq")),
        ),
        check_vma=False,
    )
```

profile of v0, /device:TPU:0, one launch (start us, length us, event | category | flops | bytes accessed | tf_op | source)
XLA Modules:
  0.0 432.6 jit_solution(1981038902537433708)
XLA Ops:
  7.2 0.7 all-gather.4.cloned.1.call-update
  7.9 0.7 all-gather.6.cloned.1.call-update
  8.7 0.7 broadcast_add_fusion
  9.4 2.3 collective-permute-start.1
  11.8 1.3 collective-permute-start.3
  13.1 26.5 %all-gather = f32[16,64,31]{1,2,0:T(8,128)S(1)} all-gather(f32[1,64,31]{1,2,0:T(8,128)} %bitcast.175), channel_id=1, replica_groups=mesh['mix'=2,'seq'=16] {'seq'}, dimensions={0}, use_global_device_ids=true | all-gather | bytes 134912 | tf_op jit(solution)/shard_map/all_gather | solution.py:39
  39.6 0.2 copy.18
  39.9 1.3 fusion.301
  41.9 0.9 dynamic-update-slice.2
  42.7 0.8 dynamic-update-slice
  43.6 30.2 %all-reduce = f32[1024]{0:T(1024)S(1)} all-reduce(f32[1024]{0:T(1024)S(1)} %dynamic-update-slice), channel_id=1, replica_groups=mesh['mix'=2,'seq'=16] {'seq'}, use_global_device_ids=true, to_apply=%add | all-reduce | flops 1024 | bytes 8192
  73.8 1.1 convert_reduce_fusion
  74.9 1.2 fusion.129
  76.2 0.9 dynamic-update-slice.1
  77.1 0.7 compare_convert_fusion.29
  77.9 3.1 fusion.291
  81.2 1.5 collective-permute-start
  82.7 1.3 collective-permute-start.2
  84.1 1.7 collective-permute-done.2
  85.8 4.7 %fusion.294 = (f32[1024]{0:T(1024)S(1)}, f32[1024]{0:T(1024)S(1)}, f32[128,1024]{1,0:T(8,128)S(1)}) fusion(f32[128]{0:T(128)S(1)} %get-tuple-element.110, bf16[15,1024]{1,0:T(8,128)(2,1)S(1)} %collective-permute-done.2, bf16[128,1024]{1,0:T(8,128)(2,1)S(1)} %multiply_convert_fusion.3, f32[1024]{0:T(1024)S(1)} %bitcast.107, f32[128]{0:T(128)S(1)} %get-tuple-element.111, ...), kind=kLoop, calls=%fused_computation.505 | loop fusion | flops 28178432 | bytes 998400 | tf_op jit(solution)/shard_map/reduce_sum | solution.py:72
  90.5 59.8 %all-reduce.5 = (f32[1024]{0:T(1024)S(1)}, f32[1024]{0:T(1024)S(1)}, f32[1024]{0:T(1024)S(1)}, f32[1024]{0:T(1024)S(1)}) all-reduce(f32[1024]{0:T(1024)S(1)} %dynamic-update-slice.2, f32[1024]{0:T(1024)S(1)} %dynamic-update-slice.1, f32[1024]{0:T(1024)S(1)} %get-tuple-element.45, ...), channel_id=1, replica_groups=mesh['mix'=2,'seq'=16] {'seq'}, use_global_device_ids=true, to_apply=%add.2 | all-reduce | flops 4096 | bytes 32768
  150.3 2.5 fusion.293
  152.8 30.0 %all-reduce.4 = (f32[1024]{0:T(1024)S(1)}, f32[1024]{0:T(1024)S(1)}) all-reduce(f32[1024]{0:T(1024)S(1)} %get-tuple-element.43, f32[1024]{0:T(1024)S(1)} %get-tuple-element.42), channel_id=1, replica_groups=mesh['mix'=2,'seq'=16] {'seq'}, use_global_device_ids=true, to_apply=%region_9.0 | all-reduce | flops 2048 | bytes 16384 | tf_op jit(solution)/shard_map/psum | solution.py:102
  182.8 0.9 fusion.250
  183.7 0.3 fusion.162
  184.0 0.4 fusion.208
  184.4 0.7 fusion.247
  185.1 0.7 fusion.180
  185.8 0.7 fusion.198
  186.5 0.2 stack.127
  186.7 1.0 copy.19
  187.8 2.7 convolution_multiply_fusion.1
  190.6 0.2 reduce-scatter.6.cloned.1.call-start
  190.8 1.3 collective-permute-start.4
  192.1 3.0 collective-permute-start.5
  195.2 0.9 collective-permute-done.5
  196.1 4.3 %multiply_convert_fusion.1 = (bf16[128,1024]{1,0:T(8,128)(2,1)S(1)}, f32[128,1024]{1,0:T(8,128)S(1)}) fusion(f32[128,2048]{1,0:T(8,128)S(1)} %fusion.291, f32[128]{0:T(128)S(1)} %get-tuple-element.94, f32[128,1024]{1,0:T(8,128)S(1)} %get-tuple-element.52, f32[15,1024]{1,0:T(8,128)S(1)} %collective-permute-done.5, f32[1024]{0:T(1024)S(1)} %bitcast.108, ...), kind=kLoop, calls=%fused_computation.415 | loop fusion | flops 16515072 | bytes 2100224 | tf_op jit(solution)/shard_map/convert
  200.4 0.2 multiply_convert_fusion
  200.6 4.6 %convolution_multiply_fusion = f32[1024,2048]{1,0:T(8,128)} fusion(bf16[128,1024]{1,0:T(8,128)(2,1)S(1)} %multiply_convert_fusion, bf16[128,1024]{1,0:T(8,128)(2,1)S(1)} %get-tuple-element.53, bf16[128,1024]{1,0:T(8,128)(2,1)S(1)} %copy-done, f32[1024]{0:T(1024)S(1)} %all-reduce, f32[128]{0:T(128)S(1)} %add_rsqrt_fusion.1, f32[128]{0:T(128)S(1)} %broadcast_multiply_fusion.6), kind=kOutput, calls=%fused_computation | convolution fusion | flops 540672000 | bytes 9180160 | tf_op jit(solution)/shard_map/fa,fb->ab/dot_general | solution.py:137
  205.9 0.6 dynamic-slice_multiply_fusion
  206.5 3.1 fusion.1
  209.6 1.6 fusion.128
  211.3 31.1 %all-reduce.3 = f32[1024]{0:T(1024)S(1)} all-reduce(f32[1024]{0:T(1024)S(1)} %broadcast_multiply_fusion.1), channel_id=5, replica_groups=mesh['mix'=2,'seq'=16] {'seq'}, use_global_device_ids=true, to_apply=%region_47.0.clone | all-reduce | flops 1024 | bytes 8192
  242.4 0.6 dynamic-slice.4
  243.0 1.0 fusion.127
  244.0 1.4 copy.20
  245.4 72.5 %reduce-scatter.8.cloned.1.call-done = f32[64,1024]{1,0:T(8,128)} async-done(((f32[1024,1024]{1,0:T(8,128)}), f32[64,1024]{1,0:T(8,128)}) %reduce-scatter.8.cloned.1.call-update) | async-done | bytes 262160 | tf_op jit(solution)/shard_map/reduce_scatter | solution.py:88
  317.9 108.2 %reduce-scatter.6.cloned.1.call-done = f32[64,2048]{1,0:T(8,128)} async-done(((f32[1024,2048]{1,0:T(8,128)}), f32[64,2048]{1,0:T(8,128)}) %reduce-scatter.6.cloned.1.call-update) | async-done | bytes 524304 | tf_op jit(solution)/shard_map/reduce_scatter | solution.py:141
  (41 shorter events, 0.9 us)
Async XLA Ops:
  7.2 70.7 %all-gather.4.cloned.1.call-start = ((), (), s32[]{:S(2)}) async-start(), calls=%async_computation.3 | async-start | bytes 4456448 | tf_op jit(solution)/shard_map/all_gather | solution.py:57
  7.9 142.4 %all-gather.6.cloned.1.call-start = ((), (), s32[]{:S(2)}) async-start(), calls=%async_computation.4 | async-start | bytes 2228224 | tf_op jit(solution)/shard_map/all_gather | solution.py:84
  8.6 235.3 %reduce-scatter.10.cloned.1.call-start = ((), (), s32[]{:S(2)}) async-start(), calls=%async_computation.7 | async-start | bytes 557056
  9.4 67.6 %collective-permute-start.1 = (s32[15]{0:T(128)S(1)}, s32[15]{0:T(128)S(1)}, u32[]{:S(2)}, u32[]{:S(2)}) collective-permute-start(s32[15]{0:T(128)S(1)} %get-tuple-element.128), channel_id=1, source_target_pairs={{0,1},{1,2},{2,3},{3,4},{4,5},{5,6},{6,7},{7,8},{8,9},{9,10},{10,1... | collective-permute-start | bytes 188 | tf_op jit(solution)/shard_map/ppermute | solution.py:19
  11.8 65.3 %collective-permute-start.3 = (s32[15]{0:T(128)S(1)}, s32[15]{0:T(128)S(1)}, u32[]{:S(2)}, u32[]{:S(2)}) collective-permute-start(s32[15]{0:T(128)S(1)} %get-tuple-element.129), channel_id=1, source_target_pairs={{1,0},{2,1},{3,2},{4,3},{5,4},{6,5},{7,6},{8,7},{9,8},{10,9},{11,1... | collective-permute-start | bytes 188 | tf_op jit(solution)/shard_map/ppermute | solution.py:21
  39.7 44.3 %copy-start.3 = (s32[128]{0:T(128)S(1)}, s32[128]{0:T(128)}, u32[]{:S(2)}) copy-start(s32[128]{0:T(128)} %param.10) | copy-start | bytes 1540
  76.1 74.2 %copy-start.2 = (bf16[128,1024]{1,0:T(8,128)(2,1)S(1)}, bf16[128,1024]{1,0:T(8,128)(2,1)}, u32[]{:S(2)}) copy-start(bf16[128,1024]{1,0:T(8,128)(2,1)} %param.11) | copy-start | bytes 786436
  81.2 2.9 collective-permute-start
  82.7 3.1 collective-permute-start.2
  187.8 130.1 %reduce-scatter.8.cloned.1.call-start = ((), (), s32[]{:S(2)}) async-start(), calls=%async_computation.6 | async-start | bytes 4456448 | tf_op jit(solution)/shard_map/reduce_scatter | solution.py:88
  190.6 10.0 %copy-start = (bf16[128,1024]{1,0:T(8,128)(2,1)S(1)}, bf16[128,1024]{1,0:T(8,128)(2,1)}, u32[]{:S(2)}) copy-start(bf16[128,1024]{1,0:T(8,128)(2,1)} %param.9) | copy-start | bytes 786436
  190.6 235.5 %reduce-scatter.6.cloned.1.call-start = ((), (), s32[]{:S(2)}) async-start(), calls=%async_computation.5 | async-start | bytes 8912896 | tf_op jit(solution)/shard_map/reduce_scatter | solution.py:141
  190.8 4.3 %collective-permute-start.4 = (f32[15,1024]{1,0:T(8,128)S(1)}, f32[15,1024]{1,0:T(8,128)S(1)}, u32[]{:S(2)}, u32[]{:S(2)}) collective-permute-start(f32[15,1024]{1,0:T(8,128)S(1)} %get-tuple-element.56), channel_id=1, source_target_pairs={{1,0},{2,1},{3,2},{4,3},{5,4},{6,5},{7,6},{8,7},{9,8},{10,9},{11,1... | collective-permute-start | bytes 184328 | tf_op jit(solution)/shard_map/ppermute | solution.py:21
  192.1 3.9 collective-permute-start.5
  205.9 3.7 copy-start.1
Sparse Core Ops, SparseCore 0:
  10.2 54.4 all-gather.3
  66.8 39.9 all-gather.5
  187.9 53.3 reduce-scatter.9
  246.1 71.7 reduce-scatter.7
  322.4 103.6 reduce-scatter.5
where the time goes:
time: 433 us
  waiting for transfers between devices  185 us (43%)
  blocking collectives  178 us (41%)
  other arithmetic  18.4 us (4%)
  matrix products  17.7 us (4%)
  between operations  15.4 us (4%)
  starting transfers between devices  11.1 us (3%)
  local copies, waits for them, and re-layouts  7.65 us (2%)
    unnamed x3, blocking collectives  121 us
    reduce_scatter x1, waiting for transfers between devices, local(): lax.psum_scatter(in_term, 'seq', scatter_dimension=0, tiled=True)  108 us
    reduce_scatter x1, waiting for transfers between devices, local(): lax.psum_scatter(jnp.einsum('fa,fb->ab', activation, out_grad, preferred_...  72.5 us
    psum x1, blocking collectives, local(): lax.psum((jnp.sum(grad_zed, axis=0), jnp.sum(grad_zed * bn_hat, axis=0)),...  30 us
    all_gather x1, blocking collectives, local(): lax.all_gather(dw_kernel, 'seq', axis=1, tiled=True)  26.5 us
  transfers between devices with their start and end apart: 11, of which 4 were waited for; matrix products, arithmetic and copies ran while one was open for 8% of the time, Pallas kernels for 0%

commit v1 on v0

--- a/solution.py
+++ b/solution.py
@@ -3,6 +3,8 @@
 import jax
 import jax.numpy as jnp
 from jax import lax
+from jax.experimental import pallas as pl
+from jax.experimental.pallas import tpu as pltpu
 from jax.sharding import PartitionSpec as P
 
 EPSILON = 1e-05
@@ -161,9 +163,553 @@
     )
 
 
+TEAM = 4
+LINE = 4
+PAD = 16
+ROWS = 64
+(
+    S_WIN,
+    S_GAIN,
+    S_FRAMES,
+    S_IDS,
+    S_OG,
+    S_WIN_Z,
+    S_GAIN_Z,
+    S_PRM,
+    S_WOUT,
+    S_IDS_HALO,
+    S_GLU_HALO,
+    S_BN,
+    S_BN_BACK,
+    S_GC_HALO,
+    S_PROJ,
+    S_GWOUT,
+    S_GK,
+    S_GWIN,
+    S_GGAIN,
+    S_GLN,
+    S_GWIN_T,
+    S_GGAIN_T,
+    STAGES,
+) = range(23)
+F32 = jnp.float32
+BF16 = jnp.bfloat16
+
+
+def fused_kernel(
+    frames_in,
+    ids_in,
+    og_in,
+    gain_in,
+    win_in,
+    prm_in,
+    wout_in,
+    out_ref,
+    gframes_ref,
+    gwin_ref,
+    gwout_ref,
+    gk_ref,
+    ggain_ref,
+    gbn_ref,
+    fr,
+    idx,
+    og,
+    gains,
+    gvec,
+    win,
+    prm,
+    prml,
+    wout,
+    lnhat,
+    rstd,
+    lnx,
+    left,
+    gate,
+    gext,
+    conv,
+    gact,
+    act,
+    bst,
+    bst2,
+    gcext,
+    gh,
+    gkacc,
+    gkr,
+    gkrecv,
+    projs,
+    projr,
+    gwos,
+    gwor,
+    gwis,
+    gwir,
+    gwit,
+    gwitr,
+    glns,
+    glnr,
+    ggs,
+    ggr,
+    ggt,
+    ggtr,
+    send_sem,
+    recv_sem,
+):
+    block, width = frames_in.shape
+    group = block * TEAM
+    chan = width // TEAM
+    share = wout_in.shape[0]
+    stream = group * LINE
+    scale = 1.0 / math.sqrt(stream)
+    me = lax.axis_index("seq")
+    z, g = me // TEAM, me % TEAM
+
+    def team(d):
+        return z * TEAM + (g + d) % TEAM
+
+    def line(d):
+        return ((z + d) % LINE) * TEAM + g
+
+    def rows(i, n):
+        return pl.ds(pl.multiple_of(i * n, n), n)
+
+    started = []
+
+    def send(stage, d, source, target, device):
+        copy = pltpu.make_async_remote_copy(
+            src_ref=source,
+            dst_ref=target,
+            send_sem=send_sem.at[stage, d],
+            recv_sem=recv_sem.at[stage, d],
+            device_id={"seq": device},
+            device_id_type=pl.DeviceIdType.MESH,
+        )
+        copy.start()
+        started.append(copy)
+        return copy
+
+    def arrive(copies):
+        for copy in copies:
+            copy.wait_recv()
+
+    order = (2, 1, 3)
+    barrier = pltpu.get_barrier_semaphore()
+    for d in (1, 2, 3):
+        for device in (team(d), line(d)):
+            pl.semaphore_signal(
+                barrier, inc=1, device_id={"seq": device}, device_id_type=pl.DeviceIdType.MESH
+            )
+    pl.semaphore_wait(barrier, 6)
+
+    c_win = [
+        send(S_WIN, d, win_in.at[(g + d) % TEAM], win.at[rows(me, share)], team(d)) for d in order
+    ]
+    c_gain = [send(S_GAIN, d, gain_in, gains.at[me], team(d)) for d in order]
+    c_prm = [send(S_PRM, d, prm_in, prm.at[z], line(d)) for d in order]
+    c_frames = [send(S_FRAMES, d, frames_in, fr.at[rows(g, block)], team(d)) for d in order]
+    ids_own = pl.ds(pl.multiple_of(PAD + g * block, PAD), block)
+    c_ids = [send(S_IDS, d, ids_in, idx.at[ids_own], team(d)) for d in order]
+    c_og = [send(S_OG, d, og_in, og.at[rows(g, block)], team(d)) for d in order]
+    win[rows(me, share)] = win_in[g]
+    gains[me] = gain_in[...]
+    prm[z] = prm_in[...]
+    fr[rows(g, block)] = frames_in[...]
+    idx[ids_own] = ids_in[...]
+    og[rows(g, block)] = og_in[...]
+    wout[rows(z, share)] = wout_in[...]
+
+    arrive(c_win)
+    win_own = rows(z, share * TEAM)
+    c_win_z = [send(S_WIN_Z, d, win.at[win_own], win.at[win_own], line(d)) for d in order]
+    arrive(c_gain)
+    team_own = pl.ds(z * TEAM, TEAM)
+    c_gain_z = [send(S_GAIN_Z, d, gains.at[team_own], gains.at[team_own], line(d)) for d in order]
+    c_wout = [send(S_WOUT, d, wout_in, wout.at[rows(z, share)], line(d)) for d in order]
+    arrive(c_ids)
+    c_idh = [
+        send(S_IDS_HALO, 1, idx.at[pl.ds(group, PAD)], idx.at[pl.ds(0, PAD)], line(1)),
+        send(S_IDS_HALO, 3, idx.at[pl.ds(PAD, PAD)], idx.at[pl.ds(PAD + group, PAD)], line(3)),
+    ]
+
+    arrive(c_gain_z)
+    for j in range(width // 128):
+        gvec[:, pl.ds(128 * j, 128)] = gains[2 * j] + gains[2 * j + 1]
+    arrive(c_frames)
+
+    @pl.loop(0, group // 32)
+    def _(i):
+        at = rows(i, 32)
+        x = fr[at].astype(F32)
+        centred = x - jnp.mean(x, axis=1, keepdims=True)
+        r = lax.rsqrt(jnp.mean(centred * centred, axis=1, keepdims=True) + EPSILON)
+        hat = centred * r
+        lnhat[at] = hat
+        rstd[at] = jnp.broadcast_to(r, (32, 128))
+        lnx[at] = (hat * gvec[0:1, :]).astype(BF16)
+
+    arrive(c_prm)
+    prml[:, 0:128] = prm[0] + prm[1]
+    prml[:, 128:256] = prm[2] + prm[3]
+    arrive(c_idh)
+
+    @pl.when(z == 0)
+    def _():
+        idx[pl.ds(0, PAD)] = jnp.full((PAD, 128), -1.0, F32)
+
+    @pl.when(z == LINE - 1)
+    def _():
+        idx[pl.ds(PAD + group, PAD)] = jnp.full((PAD, 128), -1.0, F32)
+
+    arrive(c_win_z)
+
+    @pl.loop(0, TEAM)
+    def _(i):
+        at = rows(i, block)
+        h = jnp.dot(lnx[at], win[...], preferred_element_type=F32)
+        lh = h[:, :chan]
+        rg = jax.nn.sigmoid(h[:, chan:])
+        left[at] = lh
+        gate[at] = rg
+        value = (lh * rg).astype(BF16).astype(F32)
+        inner = pl.ds(pl.multiple_of(PAD + i * block, PAD), block)
+        gext[0, inner] = value[:, :128]
+        gext[1, inner] = value[:, 128:]
+
+    def halo(stage, ext):
+        return [
+            send(
+                stage, 1, ext.at[:, pl.ds(group, PAD)], ext.at[:, pl.ds(0, PAD)], line(1)
+            ),
+            send(
+                stage, 3, ext.at[:, pl.ds(PAD, PAD)], ext.at[:, pl.ds(PAD + group, PAD)], line(3)
+            ),
+        ]
+
+    c_gh = halo(S_GLU_HALO, gext)
+    chunks = group // ROWS
+
+    def forward(c):
+        at = rows(c, ROWS)
+        own = idx[pl.ds(pl.multiple_of(PAD + c * ROWS, 8), ROWS)]
+        total = [jnp.zeros((ROWS, 128), F32) for _ in range(2)]
+        for k in range(31):
+            there = pl.ds(c * ROWS + 1 + k, ROWS)
+            same = idx[there] == own
+            for t in range(2):
+                term = jnp.where(same, gext[t, there], 0.0)
+                total[t] = total[t] + prml[k : k + 1, 128 * t : 128 * t + 128] * term
+        for t in range(2):
+            conv[at, 128 * t : 128 * t + 128] = total[t]
+
+    @pl.loop(1, chunks - 1)
+    def _(c):
+        forward(c)
+
+    arrive(c_gh)
+
+    @pl.loop(0, 2)
+    def _(c):
+        forward(c * (chunks - 1))
+
+    part_mean = jnp.sum(conv[...], axis=0, keepdims=True) / group
+    off = conv[...] - part_mean
+    bst[0, 0] = jnp.broadcast_to(part_mean, (8, chan))
+    bst[0, 1] = jnp.broadcast_to(jnp.sum(off * off, axis=0, keepdims=True), (8, chan))
+    c_bn = [send(S_BN, d, bst.at[0], bst.at[d], line(d)) for d in order]
+
+    arrive(c_wout)
+    arrive(c_og)
+
+    @pl.loop(0, TEAM)
+    def _(i):
+        at = rows(i, block)
+        gact[at] = lax.dot_general(
+            og[at], wout[...], (((1,), (1,)), ((), ())), preferred_element_type=F32
+        )
+
+    arrive(c_bn)
+    means = [bst[d, 0] for d in range(LINE)]
+    bn_mean8 = (means[0] + means[1] + means[2] + means[3]) / LINE
+    spread = jnp.zeros((8, chan), F32)
+    for d in range(LINE):
+        shift = means[d] - bn_mean8
+        spread = spread + bst[d, 1] + group * (shift * shift)
+    bn_rstd = lax.rsqrt(spread / stream + EPSILON)[0:1]
+    bn_mean = bn_mean8[0:1]
+    bn_gain = prml[31:32, :]
+    bn_bias = prml[32:33, :]
+
+    def activate(i, sums):
+        at = rows(i, ROWS)
+        hat = (conv[at] - bn_mean) * bn_rstd
+        zed = hat * bn_gain + bn_bias
+        zg = jax.nn.sigmoid(zed)
+        act[at] = (zed * zg).astype(BF16)
+        gz = gact[at] * zg * (1.0 + zed * (1.0 - zg))
+        conv[at] = hat
+        gact[at] = gz
+        fold = lambda v: jnp.sum(v.reshape(ROWS // 8, 8, chan), axis=0)
+        return sums[0] + fold(gz), sums[1] + fold(gz * hat)
+
+    zero = jnp.zeros((8, chan), F32)
+    sums = lax.fori_loop(0, chunks, activate, (zero, zero))
+    for j in range(2):
+        bst2[0, j] = jnp.broadcast_to(jnp.sum(sums[j], axis=0, keepdims=True), (8, chan))
+    c_bn2 = [send(S_BN_BACK, d, bst2.at[0], bst2.at[d], line(d)) for d in order]
+
+    arrive(c_bn2)
+    bias_total = (bst2[0, 0] + bst2[1, 0] + bst2[2, 0] + bst2[3, 0])[0:1]
+    gain_total = (bst2[0, 1] + bst2[1, 1] + bst2[2, 1] + bst2[3, 1])[0:1]
+    gbn_ref[0] = jnp.broadcast_to(gain_total * scale, (8, chan))
+    gbn_ref[1] = jnp.broadcast_to(bias_total * scale, (8, chan))
+    lead = bn_gain * bn_rstd
+    bias_mean = bias_total / stream
+    gain_mean = gain_total / stream
+
+    @pl.loop(0, chunks)
+    def _(i):
+        at = rows(i, ROWS)
+        inner = pl.ds(pl.multiple_of(PAD + i * ROWS, PAD), ROWS)
+        gc = lead * (gact[at] - bias_mean - conv[at] * gain_mean)
+        gcext[0, inner] = gc[:, :128]
+        gcext[1, inner] = gc[:, 128:]
+
+    c_gc = halo(S_GC_HALO, gcext)
+
+    @pl.loop(0, TEAM)
+    def _(i):
+        at = rows(i, block)
+        projs[i] = jnp.dot(act[at], wout[...], preferred_element_type=F32).astype(BF16)
+
+    c_proj = [send(S_PROJ, d, projs.at[(g + d) % TEAM], projr.at[d], team(d)) for d in order]
+    gwo = lax.dot_general(
+        act[...], og[...], (((0,), (0,)), ((), ())), preferred_element_type=F32
+    ).astype(BF16)
+    for j in range(LINE):
+        gwos[j] = gwo[j * share : (j + 1) * share]
+    c_gwo = [send(S_GWOUT, d, gwos.at[(z + d) % LINE], gwor.at[d], line(d)) for d in order]
+
+    gkacc[...] = jnp.zeros_like(gkacc)
+
+    def backward(c):
+        at = rows(c, ROWS)
+        inner = pl.ds(pl.multiple_of(PAD + c * ROWS, 8), ROWS)
+        own = idx[inner]
+        value = [gext[t, inner] for t in range(2)]
+        total = [jnp.zeros((ROWS, 128), F32) for _ in range(2)]
+        for j in range(31):
+            k = 30 - j
+            there = pl.ds(c * ROWS + 1 + j, ROWS)
+            same = idx[there] == own
+            for t in range(2):
+                lanes = slice(128 * t, 128 * t + 128)
+                term = jnp.where(same, gcext[t, there], 0.0)
+                total[t] = total[t] + prml[k : k + 1, lanes] * term
+                fold = jnp.sum((value[t] * term).reshape(ROWS // 8, 8, 128), axis=0)
+                gkacc[k, :, lanes] = gkacc[k, :, lanes] + fold
+        for t in range(2):
+            lanes = slice(128 * t, 128 * t + 128)
+            rg = gate[at, lanes]
+            first = total[t] * rg
+            gh[at, lanes] = first.astype(BF16)
+            gh[at, slice(chan + 128 * t, chan + 128 * t + 128)] = (
+                total[t] * left[at, lanes] * rg * (1.0 - rg)
+            ).astype(BF16)
+
+    @pl.loop(1, chunks - 1)
+    def _(c):
+        backward(c)
+
+    arrive(c_gc)
+
+    @pl.loop(0, 2)
+    def _(c):
+        backward(c * (chunks - 1))
+
+    for d in (2, 1, 3, 0):
+        to = (z + d) % LINE
+        gwis[d] = lax.dot_general(
+            lnx[:, rows(to, chan)], gh[...], (((0,), (0,)), ((), ())), preferred_element_type=F32
+        ).astype(BF16)
+        if d:
+            started_copy = send(S_GWIN, d, gwis.at[d], gwir.at[d], line(d))
+            c_gwi = [started_copy] if d == 2 else c_gwi + [started_copy]
+
+    for t in range(2):
+        gkr[t] = jnp.sum(gkacc[:, :, 128 * t : 128 * t + 128], axis=1)
+    c_gk = [send(S_GK, d, gkr.at[((z + d) % LINE) // 2], gkrecv.at[d], line(d)) for d in order]
+
+    def lower(i, total):
+        at = rows(i, block)
+        part = lax.dot_general(
+            gh[at], win[...], (((1,), (1,)), ((), ())), preferred_element_type=F32
+        )
+        glns[i] = part.astype(BF16)
+        return total + jnp.sum(part * lnhat[at], axis=0, keepdims=True)
+
+    gg = lax.fori_loop(0, TEAM, lower, jnp.zeros((1, width), F32))
+    c_gln = [send(S_GLN, d, glns.at[(g + d) % TEAM], glnr.at[d], team(d)) for d in order]
+    for j in range(LINE):
+        ggs[j] = jnp.broadcast_to(gg[:, j * chan : (j + 1) * chan], (8, chan))
+    c_gg = [send(S_GGAIN, d, ggs.at[(z + d) % LINE], ggr.at[d], line(d)) for d in order]
+
+    arrive(c_proj)
+    o = frames_in[...].astype(F32) + projs[g].astype(F32)
+    for d in (1, 2, 3):
+        o = o + projr[d].astype(F32)
+    out_ref[...] = o.astype(BF16)
+    arrive(c_gwo)
+    o = gwos[z].astype(F32)
+    for d in (1, 2, 3):
+        o = o + gwor[d].astype(F32)
+    gwout_ref[...] = o * scale
+    arrive(c_gk)
+    gk_ref[...] = (gkr[z // 2] + gkrecv[1] + gkrecv[2] + gkrecv[3]) * scale
+
+    arrive(c_gg)
+    gs = ggs[z] + ggr[1] + ggr[2] + ggr[3]
+    ggt[0] = gs[:, :128]
+    ggt[1] = gs[:, 128:]
+    c_ggt = [send(S_GGAIN_T, d, ggt.at[((g + d) % TEAM) // 2], ggtr.at[d], team(d)) for d in order]
+
+    arrive(c_gln)
+
+    @pl.loop(0, block // 32)
+    def _(i):
+        at = rows(i, 32)
+        there = pl.ds(pl.multiple_of(g * block + i * 32, 32), 32)
+        gl = glns[g, at].astype(F32)
+        for d in (1, 2, 3):
+            gl = gl + glnr[d, at].astype(F32)
+        hat = lnhat[there]
+        ghat = gl * gvec[0:1, :]
+        gx = rstd[there][:, 0:1] * (
+            ghat
+            - jnp.mean(ghat, axis=1, keepdims=True)
+            - hat * jnp.mean(ghat * hat, axis=1, keepdims=True)
+        )
+        gframes_ref[at] = (og_in[at].astype(F32) + gx).astype(BF16)
+
+    arrive(c_gwi)
+    o = gwis[0].astype(F32)
+    for d in (1, 2, 3):
+        o = o + gwir[d].astype(F32)
+    o = o.astype(BF16)
+    for j in range(TEAM):
+        gwit[j] = o[j * share : (j + 1) * share]
+    c_gwt = [send(S_GWIN_T, d, gwit.at[(g + d) % TEAM], gwitr.at[d], team(d)) for d in order]
+    arrive(c_ggt)
+    ggain_ref[...] = (ggt[g // 2] + ggtr[1] + ggtr[2] + ggtr[3]) * scale
+    gwin_ref[g] = gwit[g].astype(F32) * scale
+    arrive(c_gwt)
+    for d in (1, 2, 3):
+        gwin_ref[(g + TEAM - d) % TEAM] = gwitr[d].astype(F32) * scale
+    for copy in started:
+        copy.wait_send()
+
+
+def fused(frames, segment_ids, out_grad, ln_gain, w_in, dw_kernel, bn_gain, bn_bias, w_out):
+    block, width = frames.shape
+    share = w_in.shape[0]
+    group = block * TEAM
+    chan = width // TEAM
+    me = lax.axis_index("seq")
+    z, g = me // TEAM, me % TEAM
+    ids = jnp.broadcast_to(segment_ids.astype(F32)[:, None], (block, 128))
+    lane_half = jnp.arange(128) // share
+
+    def halves(rows_, odd):
+        both = jnp.concatenate([rows_, rows_], axis=1)
+        return jnp.where(lane_half[None, :] == odd, both, 0.0)
+
+    gain = halves(jnp.broadcast_to(ln_gain[None, :], (8, share)), g % 2)
+    prm = halves(
+        jnp.concatenate(
+            [dw_kernel, bn_gain[None], bn_bias[None], jnp.zeros((7, share), F32)], axis=0
+        ),
+        z % 2,
+    )
+    win = (
+        w_in.reshape(share, 2, LINE, TEAM, share)
+        .transpose(3, 0, 1, 2, 4)
+        .reshape(TEAM, share, 2 * chan)
+    )
+    vmem = pl.BlockSpec(memory_space=pltpu.VMEM)
+    shape = jax.ShapeDtypeStruct
+    ext = group + 2 * PAD
+    out, gframes, gwin, gwout, gk, ggain, gbn = pl.pallas_call(
+        fused_kernel,
+        out_shape=[
+            shape((block, width), BF16),
+            shape((block, width), BF16),
+            shape((TEAM, share, 2 * chan), F32),
+            shape((share, width), F32),
+            shape((32, 128), F32),
+            shape((8, 128), F32),
+            shape((2, 8, chan), F32),
+        ],
+        in_specs=[vmem] * 7,
+        out_specs=[vmem] * 7,
+        scratch_shapes=[
+            pltpu.VMEM((group, width), BF16),
+            pltpu.VMEM((ext, 128), F32),
+            pltpu.VMEM((group, width), BF16),
+            pltpu.VMEM((TEAM * LINE, 8, 128), F32),
+            pltpu.VMEM((8, width), F32),
+            pltpu.VMEM((width, 2 * chan), BF16),
+            pltpu.VMEM((LINE, 40, 128), F32),
+            pltpu.VMEM((40, chan), F32),
+            pltpu.VMEM((chan, width), BF16),
+            pltpu.VMEM((group, width), F32),
+            pltpu.VMEM((group, 128), F32),
+            pltpu.VMEM((group, width), BF16),
+            pltpu.VMEM((group, chan), F32),
+            pltpu.VMEM((group, chan), F32),
+            pltpu.VMEM((2, ext, 128), F32),
+            pltpu.VMEM((group, chan), F32),
+            pltpu.VMEM((group, chan), F32),
+            pltpu.VMEM((group, chan), BF16),
+            pltpu.VMEM((LINE, 2, 8, chan), F32),
+            pltpu.VMEM((LINE, 2, 8, chan), F32),
+            pltpu.VMEM((2, ext, 128), F32),
+            pltpu.VMEM((group, 2 * chan), BF16),
+            pltpu.VMEM((32, 8, chan), F32),
+            pltpu.VMEM((2, 32, 128), F32),
+            pltpu.VMEM((LINE, 32, 128), F32),
+            pltpu.VMEM((TEAM, block, width), BF16),
+            pltpu.VMEM((TEAM, block, width), BF16),
+            pltpu.VMEM((LINE, share, width), BF16),
+            pltpu.VMEM((LINE, share, width), BF16),
+            pltpu.VMEM((LINE, chan, 2 * chan), BF16),
+            pltpu.VMEM((LINE, chan, 2 * chan), BF16),
+            pltpu.VMEM((TEAM, share, 2 * chan), BF16),
+            pltpu.VMEM((TEAM, share, 2 * chan), BF16),
+            pltpu.VMEM((TEAM, block, width), BF16),
+            pltpu.VMEM((TEAM, block, width), BF16),
+            pltpu.VMEM((LINE, 8, chan), F32),
+            pltpu.VMEM((LINE, 8, chan), F32),
+            pltpu.VMEM((2, 8, 128), F32),
+            pltpu.VMEM((TEAM, 8, 128), F32),
+            pltpu.SemaphoreType.DMA((STAGES, 4)),
+            pltpu.SemaphoreType.DMA((STAGES, 4)),
+        ],
+        compiler_params=pltpu.CompilerParams(
+            collective_id=0, has_side_effects=True, vmem_limit_bytes=48 * 1024 * 1024
+        ),
+    )(frames, ids, out_grad, gain, win, prm, w_out)
+    gwin = (
+        gwin.reshape(TEAM, share, 2, LINE, share)
+        .transpose(1, 2, 3, 0, 4)
+        .reshape(share, 2 * width)
+    )
+    gk = jnp.where(z % 2 == 0, gk[:31, :share], gk[:31, share:])
+    ggain = jnp.where(g % 2 == 0, ggain[0, :share], ggain[0, share:])
+    gbn = lax.dynamic_slice_in_dim(gbn[:, 0, :], z * share, share, 1)
+    return out, gframes, gwin, gwout, gk, ggain, gbn[0], gbn[1]
+
+
 def solution(mesh):
+    small = mesh.shape["seq"] == TEAM * LINE
     return jax.shard_map(
-        local,
+        fused if small else local,
         mesh=mesh,
         in_specs=(
             P(("mix", "seq"), None),

time: 433 us -> 114 us (0.26)
  waiting for transfers between devices: 185 us -> 0 us
  blocking collectives: 178 us -> 0 us
  Pallas kernels: 0 us -> 102 us
  matrix products: 17.7 us -> 0 us
  other arithmetic: 18.4 us -> 1.43 us
  between operations: 15.4 us -> 0.79 us
  starting transfers between devices: 11.1 us -> 0 us
    reduce_scatter x2 -> x0, waiting for transfers between devices: 181 us -> none  [the longest x1 108 us: local(): lax.psum_scatter(in_term, 'seq', scatter_dimension=0, tiled=True)]
    unnamed x3 -> x0, blocking collectives: 121 us -> none
    pallas_call x0 -> x1, Pallas kernels: none -> 102 us  [fused(): pl.pallas_call(fused_kernel, out_shape=[shape((block, width), BF16), shap...]
    psum x1 -> x0, blocking collectives: 30 us -> none  [local(): lax.psum((jnp.sum(grad_zed, axis=0), jnp.sum(grad_zed * bn_hat, axis=0)),...]
    all_gather x1 -> x0, blocking collectives: 26.5 us -> none  [local(): lax.all_gather(dw_kernel, 'seq', axis=1, tiled=True)]
    dot_general x6 -> x0, matrix products: 17.7 us -> none  [the longest x1 4.6 us: local(): jnp.einsum('fa,fb->ab', ln_x, grad_hidden, preferred_element_type=jnp.flo...]
    ppermute x6 -> x0, starting transfers between devices: 10.8 us -> none  [the longest x3 6.9 us: with_halo(): lax.ppermute(tail, axis, [(i, (i + 1) % count) for i in range(ends)])]
    reduce_sum x9 -> x0, other arithmetic: 10.5 us -> none  [the longest x1 4.67 us: local(): jnp.sum(conv_out, axis=0)]
  transfers between devices with their start and end apart: 11 -> 0, of which waited for: 4 -> 0; matrix products, arithmetic and copies ran while one was open for 8% -> 0% of each run, Pallas kernels for 0% -> 0%
where the time goes in v1:
time: 114 us
  Pallas kernels  102 us (89%)
  local copies, waits for them, and re-layouts  9.58 us (8%)
  other arithmetic  1.43 us (1%)
    pallas_call x1, Pallas kernels, fused(): pl.pallas_call(fused_kernel, out_shape=[shape((block, width), BF16), shap...  102 us
    unnamed x19, local copies, waits for them, and re-layouts  4.11 us

profile of v1, /device:TPU:0, one launch (start us, length us, event | category | flops | bytes accessed | tf_op | source)
XLA Modules:
  0.0 113.6 jit_solution(5526594971994593901)
XLA Ops:
  0.7 0.0 copy-start.7
  0.7 0.0 copy-start.6
  0.7 0.0 copy-start.3
  0.7 0.6 copy-done.7
  1.3 0.0 copy-done.6
  1.4 0.1 maximum_select_fusion.1.gain_in
  1.4 0.0 copy-start.4
  1.4 0.0 copy-start.5
  1.4 0.0 copy-done.3
  1.5 0.6 copy-done.4
  2.1 0.0 copy-done.5
  2.1 0.1 maximum_select_fusion.prm_in
  2.2 0.1 broadcast_in_dim.47.ids_in
  2.3 1.5 %reshape.56 = bf16[64,2,4,4,64]{4,3,2,1,0:T(4,128)(2,1)S(1)} reshape(bf16[64,2048]{1,0:T(8,128)(2,1)} %param.13) | data formatting | bytes 524288 | tf_op jit(solution)/shard_map/reshape | solution.py:631
  3.7 0.2 copy.20
  4.0 0.0 copy-start
  4.0 0.0 copy-start.1
  4.0 0.0 copy-start.2
  4.0 0.3 reshape.57.win_in
  4.3 0.6 copy-done
  4.9 0.1 copy-done.1
  5.0 0.0 copy-done.2
  5.0 101.8 %shard_map.152 = (bf16[128,1024]{1,0:T(8,128)(2,1)S(1)}, bf16[128,1024]{1,0:T(8,128)(2,1)S(1)}, f32[4,64,512]{2,1,0:T(8,128)S(1)}, f32[64,1024]{1,0:T(8,128)S(1)...) custom-call(bf16[128,1024]{1,0:T(8,128)(2,1)S(1)} %copy-done, ...), custom_call_target="tpu_custom_call" | custom-call | tf_op jit(solution)/shard_map/pallas_call | solution.py:638
  106.8 0.6 fusion
  107.4 0.6 dynamic-slice_bitcast_fusion
  108.0 0.7 slice_select_fusion
  108.6 0.5 reshape.58
  109.2 0.7 copy.18
  109.9 1.6 %reshape.59 = f32[64,2048]{1,0:T(8,128)} reshape(f32[64,2,4,4,64]{4,3,2,1,0:T(4,128)S(1)} %copy.18) | data formatting | bytes 1048576 | tf_op jit(solution)/shard_map/reshape | solution.py:701
  111.5 0.7 copy.24
  112.2 0.7 copy.25
  112.9 0.7 copy.26
  (5 shorter events, 0.0 us)
Async XLA Ops:
  0.7 0.7 copy-start.7
  0.7 0.7 copy-start.6
  0.7 0.7 copy-start.3
  1.4 0.7 copy-start.4
  1.4 0.7 copy-start.5
  4.0 1.0 copy-start
  4.0 1.0 copy-start.1
  4.0 1.0 copy-start.2

commit v2 on v1

--- a/solution.py
+++ b/solution.py
@@ -190,8 +190,10 @@
     S_GLN,
     S_GWIN_T,
     S_GGAIN_T,
+    S_GWIN_B,
+    S_GWIN_TB,
     STAGES,
-) = range(23)
+) = range(25)
 F32 = jnp.float32
 BF16 = jnp.bfloat16
 
@@ -233,6 +235,8 @@
     bst2,
     gcext,
     gh,
+    hs,
+    hr,
     gkacc,
     gkr,
     gkrecv,
@@ -303,32 +307,31 @@
         send(S_WIN, d, win_in.at[(g + d) % TEAM], win.at[rows(me, share)], team(d)) for d in order
     ]
     c_gain = [send(S_GAIN, d, gain_in, gains.at[me], team(d)) for d in order]
-    c_prm = [send(S_PRM, d, prm_in, prm.at[z], line(d)) for d in order]
+    win[rows(me, share)] = win_in[g]
+    gains[me] = gain_in[...]
+    arrive(c_win)
+    win_own = rows(z, share * TEAM)
+    c_win_z = [send(S_WIN_Z, d, win.at[win_own], win.at[win_own], line(d)) for d in order]
     c_frames = [send(S_FRAMES, d, frames_in, fr.at[rows(g, block)], team(d)) for d in order]
+    arrive(c_gain)
+    team_own = pl.ds(z * TEAM, TEAM)
+    c_gain_z = [send(S_GAIN_Z, d, gains.at[team_own], gains.at[team_own], line(d)) for d in order]
     ids_own = pl.ds(pl.multiple_of(PAD + g * block, PAD), block)
     c_ids = [send(S_IDS, d, ids_in, idx.at[ids_own], team(d)) for d in order]
-    c_og = [send(S_OG, d, og_in, og.at[rows(g, block)], team(d)) for d in order]
-    win[rows(me, share)] = win_in[g]
-    gains[me] = gain_in[...]
+    c_prm = [send(S_PRM, d, prm_in, prm.at[z], line(d)) for d in order]
     prm[z] = prm_in[...]
     fr[rows(g, block)] = frames_in[...]
     idx[ids_own] = ids_in[...]
     og[rows(g, block)] = og_in[...]
     wout[rows(z, share)] = wout_in[...]
-
-    arrive(c_win)
-    win_own = rows(z, share * TEAM)
-    c_win_z = [send(S_WIN_Z, d, win.at[win_own], win.at[win_own], line(d)) for d in order]
-    arrive(c_gain)
-    team_own = pl.ds(z * TEAM, TEAM)
-    c_gain_z = [send(S_GAIN_Z, d, gains.at[team_own], gains.at[team_own], line(d)) for d in order]
-    c_wout = [send(S_WOUT, d, wout_in, wout.at[rows(z, share)], line(d)) for d in order]
     arrive(c_ids)
     c_idh = [
         send(S_IDS_HALO, 1, idx.at[pl.ds(group, PAD)], idx.at[pl.ds(0, PAD)], line(1)),
         send(S_IDS_HALO, 3, idx.at[pl.ds(PAD, PAD)], idx.at[pl.ds(PAD + group, PAD)], line(3)),
     ]
 
+    c_og = [send(S_OG, d, og_in, og.at[rows(g, block)], team(d)) for d in order]
+    c_wout = [send(S_WOUT, d, wout_in, wout.at[rows(z, share)], line(d)) for d in order]
     arrive(c_gain_z)
     for j in range(width // 128):
         gvec[:, pl.ds(128 * j, 128)] = gains[2 * j] + gains[2 * j + 1]
@@ -364,14 +367,14 @@
     def _(i):
         at = rows(i, block)
         h = jnp.dot(lnx[at], win[...], preferred_element_type=F32)
-        lh = h[:, :chan]
-        rg = jax.nn.sigmoid(h[:, chan:])
-        left[at] = lh
-        gate[at] = rg
-        value = (lh * rg).astype(BF16).astype(F32)
         inner = pl.ds(pl.multiple_of(PAD + i * block, PAD), block)
-        gext[0, inner] = value[:, :128]
-        gext[1, inner] = value[:, 128:]
+        for t in range(2):
+            lanes = slice(128 * t, 128 * t + 128)
+            lh = h[:, 256 * t : 256 * t + 128]
+            rg = jax.nn.sigmoid(h[:, 256 * t + 128 : 256 * t + 256])
+            left[at, lanes] = lh
+            gate[at, lanes] = rg
+            gext[t, inner] = (lh * rg).astype(BF16).astype(F32)
 
     def halo(stage, ext):
         return [
@@ -455,6 +458,28 @@
         bst2[0, j] = jnp.broadcast_to(jnp.sum(sums[j], axis=0, keepdims=True), (8, chan))
     c_bn2 = [send(S_BN_BACK, d, bst2.at[0], bst2.at[d], line(d)) for d in order]
 
+    for j in range(2):
+        edge = slice(j * (group - PAD), j * (group - PAD) + PAD)
+        hs[j, 0] = gact[edge]
+        hs[j, 1] = conv[edge]
+    c_gc = [
+        send(S_GC_HALO, 1, hs.at[1], hr.at[0], line(1)),
+        send(S_GC_HALO, 3, hs.at[0], hr.at[1], line(3)),
+    ]
+    gwo = lax.dot_general(
+        act[...], og[...], (((0,), (0,)), ((), ())), preferred_element_type=F32
+    ).astype(BF16)
+    for j in range(LINE):
+        gwos[j] = gwo[j * share : (j + 1) * share]
+    c_gwo = [send(S_GWOUT, d, gwos.at[(z + d) % LINE], gwor.at[d], line(d)) for d in order]
+
+    @pl.loop(0, TEAM)
+    def _(i):
+        at = rows(i, block)
+        projs[i] = jnp.dot(act[at], wout[...], preferred_element_type=F32).astype(BF16)
+
+    c_proj = [send(S_PROJ, d, projs.at[(g + d) % TEAM], projr.at[d], team(d)) for d in order]
+
     arrive(c_bn2)
     bias_total = (bst2[0, 0] + bst2[1, 0] + bst2[2, 0] + bst2[3, 0])[0:1]
     gain_total = (bst2[0, 1] + bst2[1, 1] + bst2[2, 1] + bst2[3, 1])[0:1]
@@ -464,74 +489,62 @@
     bias_mean = bias_total / stream
     gain_mean = gain_total / stream
 
+    def store_gc(inner, grad, hat):
+        gc = lead * (grad - bias_mean - hat * gain_mean)
+        gcext[0, inner] = gc[:, :128]
+        gcext[1, inner] = gc[:, 128:]
+
     @pl.loop(0, chunks)
     def _(i):
         at = rows(i, ROWS)
-        inner = pl.ds(pl.multiple_of(PAD + i * ROWS, PAD), ROWS)
-        gc = lead * (gact[at] - bias_mean - conv[at] * gain_mean)
-        gcext[0, inner] = gc[:, :128]
-        gcext[1, inner] = gc[:, 128:]
-
-    c_gc = halo(S_GC_HALO, gcext)
-
-    @pl.loop(0, TEAM)
-    def _(i):
-        at = rows(i, block)
-        projs[i] = jnp.dot(act[at], wout[...], preferred_element_type=F32).astype(BF16)
-
-    c_proj = [send(S_PROJ, d, projs.at[(g + d) % TEAM], projr.at[d], team(d)) for d in order]
-    gwo = lax.dot_general(
-        act[...], og[...], (((0,), (0,)), ((), ())), preferred_element_type=F32
-    ).astype(BF16)
-    for j in range(LINE):
-        gwos[j] = gwo[j * share : (j + 1) * share]
-    c_gwo = [send(S_GWOUT, d, gwos.at[(z + d) % LINE], gwor.at[d], line(d)) for d in order]
+        store_gc(pl.ds(pl.multiple_of(PAD + i * ROWS, PAD), ROWS), gact[at], conv[at])
+
+    arrive(c_gc)
+    store_gc(pl.ds(0, PAD), hr[0, 0], hr[0, 1])
+    store_gc(pl.ds(PAD + group, PAD), hr[1, 0], hr[1, 1])
 
     gkacc[...] = jnp.zeros_like(gkacc)
 
-    def backward(c):
+    def backward(c, t):
         at = rows(c, ROWS)
         inner = pl.ds(pl.multiple_of(PAD + c * ROWS, 8), ROWS)
+        lanes = slice(128 * t, 128 * t + 128)
         own = idx[inner]
-        value = [gext[t, inner] for t in range(2)]
-        total = [jnp.zeros((ROWS, 128), F32) for _ in range(2)]
+        value = gext[t, inner]
+        total = jnp.zeros((ROWS, 128), F32)
         for j in range(31):
             k = 30 - j
             there = pl.ds(c * ROWS + 1 + j, ROWS)
-            same = idx[there] == own
-            for t in range(2):
-                lanes = slice(128 * t, 128 * t + 128)
-                term = jnp.where(same, gcext[t, there], 0.0)
-                total[t] = total[t] + prml[k : k + 1, lanes] * term
-                fold = jnp.sum((value[t] * term).reshape(ROWS // 8, 8, 128), axis=0)
-                gkacc[k, :, lanes] = gkacc[k, :, lanes] + fold
-        for t in range(2):
-            lanes = slice(128 * t, 128 * t + 128)
-            rg = gate[at, lanes]
-            first = total[t] * rg
-            gh[at, lanes] = first.astype(BF16)
-            gh[at, slice(chan + 128 * t, chan + 128 * t + 128)] = (
-                total[t] * left[at, lanes] * rg * (1.0 - rg)
+            term = jnp.where(idx[there] == own, gcext[t, there], 0.0)
+            total = total + prml[k : k + 1, lanes] * term
+            fold = jnp.sum((value * term).reshape(ROWS // 8, 8, 128), axis=0)
+            gkacc[k, :, lanes] = gkacc[k, :, lanes] + fold
+        rg = gate[at, lanes]
+        gh[at, 256 * t : 256 * t + 128] = (total * rg).astype(BF16)
+        gh[at, 256 * t + 128 : 256 * t + 256] = (total * left[at, lanes] * rg * (1.0 - rg)).astype(
+            BF16
+        )
+
+    c_gwi = []
+    for t in range(2):
+
+        @pl.loop(0, chunks)
+        def _(c):
+            backward(c, t)
+
+        copies = []
+        for d in (2, 1, 3, 0):
+            gwis[t, d] = lax.dot_general(
+                lnx[:, rows((z + d) % LINE, chan)],
+                gh[:, 256 * t : 256 * t + 256],
+                (((0,), (0,)), ((), ())),
+                preferred_element_type=F32,
             ).astype(BF16)
-
-    @pl.loop(1, chunks - 1)
-    def _(c):
-        backward(c)
-
-    arrive(c_gc)
-
-    @pl.loop(0, 2)
-    def _(c):
-        backward(c * (chunks - 1))
-
-    for d in (2, 1, 3, 0):
-        to = (z + d) % LINE
-        gwis[d] = lax.dot_general(
-            lnx[:, rows(to, chan)], gh[...], (((0,), (0,)), ((), ())), preferred_element_type=F32
-        ).astype(BF16)
-        if d:
-            started_copy = send(S_GWIN, d, gwis.at[d], gwir.at[d], line(d))
-            c_gwi = [started_copy] if d == 2 else c_gwi + [started_copy]
+            if d:
+                copies.append(
+                    send((S_GWIN, S_GWIN_B)[t], d, gwis.at[t, d], gwir.at[t, d], line(d))
+                )
+        c_gwi.append(copies)
 
     for t in range(2):
         gkr[t] = jnp.sum(gkacc[:, :, 128 * t : 128 * t + 128], axis=1)
@@ -588,20 +601,41 @@
         )
         gframes_ref[at] = (og_in[at].astype(F32) + gx).astype(BF16)
 
-    arrive(c_gwi)
-    o = gwis[0].astype(F32)
-    for d in (1, 2, 3):
-        o = o + gwir[d].astype(F32)
-    o = o.astype(BF16)
-    for j in range(TEAM):
-        gwit[j] = o[j * share : (j + 1) * share]
-    c_gwt = [send(S_GWIN_T, d, gwit.at[(g + d) % TEAM], gwitr.at[d], team(d)) for d in order]
+    c_gwt = []
+    for t in range(2):
+        arrive(c_gwi[t])
+        o = gwis[t, 0].astype(F32)
+        for d in (1, 2, 3):
+            o = o + gwir[t, d].astype(F32)
+        o = o.astype(BF16)
+        for j in range(TEAM):
+            gwit[t, j] = o[j * share : (j + 1) * share]
+        c_gwt += [
+            send(
+                (S_GWIN_T, S_GWIN_TB)[t],
+                d,
+                gwit.at[t, (g + d) % TEAM],
+                gwitr.at[t, g],
+                team(d),
+            )
+            for d in order
+        ]
+        gwitr[t, g] = gwit[t, g]
     arrive(c_ggt)
     ggain_ref[...] = (ggt[g // 2] + ggtr[1] + ggtr[2] + ggtr[3]) * scale
-    gwin_ref[g] = gwit[g].astype(F32) * scale
     arrive(c_gwt)
-    for d in (1, 2, 3):
-        gwin_ref[(g + TEAM - d) % TEAM] = gwitr[d].astype(F32) * scale
+    low = lax.broadcasted_iota(jnp.int32, (share, 128), 1) < share
+    for t in range(2):
+        for half in range(2):
+            lanes = slice(128 * half, 128 * half + 128)
+            for p in range(2):
+                even = gwitr[t, 2 * p][:, lanes].astype(F32) * scale
+                odd = gwitr[t, 2 * p + 1][:, lanes].astype(F32) * scale
+                at = half * width + 2 * t * chan + 128 * p
+                gwin_ref[:, at : at + 128] = jnp.where(low, even, pltpu.roll(odd, share, 1))
+                gwin_ref[:, at + chan : at + chan + 128] = jnp.where(
+                    low, pltpu.roll(even, share, 1), odd
+                )
     for copy in started:
         copy.wait_send()
 
@@ -628,8 +662,8 @@
         z % 2,
     )
     win = (
-        w_in.reshape(share, 2, LINE, TEAM, share)
-        .transpose(3, 0, 1, 2, 4)
+        w_in.reshape(share, 2, 2, 2, TEAM, share)
+        .transpose(4, 0, 2, 1, 3, 5)
         .reshape(TEAM, share, 2 * chan)
     )
     vmem = pl.BlockSpec(memory_space=pltpu.VMEM)
@@ -640,7 +674,7 @@
         out_shape=[
             shape((block, width), BF16),
             shape((block, width), BF16),
-            shape((TEAM, share, 2 * chan), F32),
+            shape((share, 2 * width), F32),
             shape((share, width), F32),
             shape((32, 128), F32),
             shape((8, 128), F32),
@@ -671,6 +705,8 @@
             pltpu.VMEM((LINE, 2, 8, chan), F32),
             pltpu.VMEM((2, ext, 128), F32),
             pltpu.VMEM((group, 2 * chan), BF16),
+            pltpu.VMEM((2, 2, PAD, chan), F32),
+            pltpu.VMEM((2, 2, PAD, chan), F32),
             pltpu.VMEM((32, 8, chan), F32),
             pltpu.VMEM((2, 32, 128), F32),
             pltpu.VMEM((LINE, 32, 128), F32),
@@ -678,10 +714,10 @@
             pltpu.VMEM((TEAM, block, width), BF16),
             pltpu.VMEM((LINE, share, width), BF16),
             pltpu.VMEM((LINE, share, width), BF16),
-            pltpu.VMEM((LINE, chan, 2 * chan), BF16),
-            pltpu.VMEM((LINE, chan, 2 * chan), BF16),
-            pltpu.VMEM((TEAM, share, 2 * chan), BF16),
-            pltpu.VMEM((TEAM, share, 2 * chan), BF16),
+            pltpu.VMEM((2, LINE, chan, chan), BF16),
+            pltpu.VMEM((2, LINE, chan, chan), BF16),
+            pltpu.VMEM((2, TEAM, share, chan), BF16),
+            pltpu.VMEM((2, TEAM, share, chan), BF16),
             pltpu.VMEM((TEAM, block, width), BF16),
             pltpu.VMEM((TEAM, block, width), BF16),
             pltpu.VMEM((LINE, 8, chan), F32),
@@ -695,11 +731,6 @@
             collective_id=0, has_side_effects=True, vmem_limit_bytes=48 * 1024 * 1024
         ),
     )(frames, ids, out_grad, gain, win, prm, w_out)
-    gwin = (
-        gwin.reshape(TEAM, share, 2, LINE, share)
-        .transpose(1, 2, 3, 0, 4)
-        .reshape(share, 2 * width)
-    )
     gk = jnp.where(z % 2 == 0, gk[:31, :share], gk[:31, share:])
     ggain = jnp.where(g % 2 == 0, ggain[0, :share], ggain[0, share:])
     gbn = lax.dynamic_slice_in_dim(gbn[:, 0, :], z * share, share, 1)

time: 114 us -> 110 us (0.965)
  Pallas kernels: 102 us -> 99.4 us
  local copies, waits for them, and re-layouts: 9.58 us -> 7.78 us
    pallas_call x1, Pallas kernels: 102 us -> 99.4 us  [fused(): pl.pallas_call(fused_kernel, out_shape=[shape((block, width), BF16), shap...]
    reshape x5 -> x3, local copies, waits for them, and re-layouts: 4.13 us -> 2.21 us  [the longest x2 1.89 us: fused(): w_in.reshape(share, 2, 2, 2, TEAM, share).transpose(4, 0, 2, 1, 3, 5)]
    unnamed x19 -> x20, local copies, waits for them, and re-layouts: 4.11 us -> 4.9 us
where the time goes in v2:
time: 110 us; the launch traced here: 109 us
  Pallas kernels  99.4 us (90%)
  local copies, waits for them, and re-layouts  7.78 us (7%)
  other arithmetic  1.43 us (1%)
    pallas_call x1, Pallas kernels, fused(): pl.pallas_call(fused_kernel, out_shape=[shape((block, width), BF16), shap...  99.4 us
    unnamed x20, local copies, waits for them, and re-layouts  4.9 us

profile of v2, /device:TPU:0, one launch (start us, length us, event | category | flops | bytes accessed | tf_op | source)
XLA Modules:
  0.0 109.4 jit_solution(2732836986968673363)
XLA Ops:
  0.7 0.0 copy-start.7
  0.7 0.0 copy-start.6
  0.7 0.0 copy-start.3
  0.7 0.6 copy-done.7
  1.3 0.0 copy-done.6
  1.4 0.1 maximum_select_fusion.1.gain_in
  1.4 0.0 copy-start.4
  1.4 0.0 copy-start.5
  1.4 0.0 copy-done.3
  1.5 0.6 copy-done.4
  2.1 0.0 copy-done.5
  2.1 0.1 maximum_select_fusion.prm_in
  2.2 0.1 broadcast_in_dim.47.ids_in
  2.3 1.5 %reshape.50 = bf16[64,2,2,2,4,64]{5,4,3,2,1,0:T(4,128)(2,1)S(1)} reshape(bf16[64,2048]{1,0:T(8,128)(2,1)} %param.13) | data formatting | bytes 524288 | tf_op jit(solution)/shard_map/reshape | solution.py:665
  3.7 0.4 copy.19
  4.2 0.0 copy-start
  4.2 0.0 copy-start.1
  4.2 0.0 copy-start.2
  4.2 0.3 reshape.51.win_in
  4.5 0.6 copy-done
  5.1 0.1 copy-done.1
  5.2 0.0 copy-done.2
  5.2 99.4 %shard_map.152 = (bf16[128,1024]{1,0:T(8,128)(2,1)S(1)}, bf16[128,1024]{1,0:T(8,128)(2,1)S(1)}, f32[64,2048]{1,0:T(8,128)S(1)}, f32[64,1024]{1,0:T(8,128)S(1)}, ...) custom-call(bf16[128,1024]{1,0:T(8,128)(2,1)S(1)} %copy-done, ...), custom_call_target="tpu_custom_call" | custom-call | tf_op jit(solution)/shard_map/pallas_call | solution.py:672
  104.6 0.6 fusion
  105.2 0.6 dynamic-slice_bitcast_fusion
  105.8 0.7 slice_select_fusion
  106.5 0.7 copy.24
  107.2 0.7 copy.25
  107.9 0.8 copy.26
  108.7 0.7 copy.27
  (5 shorter events, 0.0 us)
Async XLA Ops:
  0.7 0.7 copy-start.7
  0.7 0.7 copy-start.6
  0.7 0.7 copy-start.3
  1.4 0.7 copy-start.4
  1.4 0.7 copy-start.5
  4.2 1.0 copy-start
  4.2 1.0 copy-start.1
  4.2 1.0 copy-start.2

commit v3 on v2

--- a/solution.py
+++ b/solution.py
@@ -330,12 +330,11 @@
         send(S_IDS_HALO, 3, idx.at[pl.ds(PAD, PAD)], idx.at[pl.ds(PAD + group, PAD)], line(3)),
     ]
 
-    c_og = [send(S_OG, d, og_in, og.at[rows(g, block)], team(d)) for d in order]
-    c_wout = [send(S_WOUT, d, wout_in, wout.at[rows(z, share)], line(d)) for d in order]
     arrive(c_gain_z)
     for j in range(width // 128):
         gvec[:, pl.ds(128 * j, 128)] = gains[2 * j] + gains[2 * j + 1]
     arrive(c_frames)
+    c_og = [send(S_OG, d, og_in, og.at[rows(g, block)], team(d)) for d in order]
 
     @pl.loop(0, group // 32)
     def _(i):
@@ -362,6 +361,7 @@
         idx[pl.ds(PAD + group, PAD)] = jnp.full((PAD, 128), -1.0, F32)
 
     arrive(c_win_z)
+    c_wout = [send(S_WOUT, d, wout_in, wout.at[rows(z, share)], line(d)) for d in order]
 
     @pl.loop(0, TEAM)
     def _(i):

time: 110 us -> 113 us (1.027)
  Pallas kernels: 99.4 us -> 103 us
    pallas_call x1, Pallas kernels: 99.4 us -> 103 us  [fused(): pl.pallas_call(fused_kernel, out_shape=[shape((block, width), BF16), shap...]
where the time goes in v3:
time: 113 us
  Pallas kernels  103 us (91%)
  local copies, waits for them, and re-layouts  7.78 us (7%)
  other arithmetic  1.43 us (1%)
    pallas_call x1, Pallas kernels, fused(): pl.pallas_call(fused_kernel, out_shape=[shape((block, width), BF16), shap...  103 us
    unnamed x20, local copies, waits for them, and re-layouts  4.9 us

profile of v3, /device:TPU:0, one launch (start us, length us, event | category | flops | bytes accessed | tf_op | source)
XLA Modules:
  0.0 112.6 jit_solution(11301346680604174608)
XLA Ops:
  0.7 0.0 copy-start.7
  0.7 0.0 copy-start.6
  0.7 0.0 copy-start.3
  0.7 0.6 copy-done.7
  1.3 0.0 copy-done.6
  1.4 0.1 maximum_select_fusion.1.gain_in
  1.4 0.0 copy-start.4
  1.4 0.0 copy-start.5
  1.4 0.0 copy-done.3
  1.5 0.6 copy-done.4
  2.1 0.0 copy-done.5
  2.1 0.1 maximum_select_fusion.prm_in
  2.2 0.1 broadcast_in_dim.47.ids_in
  2.3 1.5 %reshape.50 = bf16[64,2,2,2,4,64]{5,4,3,2,1,0:T(4,128)(2,1)S(1)} reshape(bf16[64,2048]{1,0:T(8,128)(2,1)} %param.13) | data formatting | bytes 524288 | tf_op jit(solution)/shard_map/reshape | solution.py:665
  3.7 0.4 copy.19
  4.2 0.0 copy-start
  4.2 0.0 copy-start.1
  4.2 0.0 copy-start.2
  4.2 0.3 reshape.51.win_in
  4.5 0.6 copy-done
  5.1 0.1 copy-done.1
  5.2 0.0 copy-done.2
  5.2 102.6 %shard_map.152 = (bf16[128,1024]{1,0:T(8,128)(2,1)S(1)}, bf16[128,1024]{1,0:T(8,128)(2,1)S(1)}, f32[64,2048]{1,0:T(8,128)S(1)}, f32[64,1024]{1,0:T(8,128)S(1)}, ...) custom-call(bf16[128,1024]{1,0:T(8,128)(2,1)S(1)} %copy-done, ...), custom_call_target="tpu_custom_call" | custom-call | tf_op jit(solution)/shard_map/pallas_call | solution.py:672
  107.8 0.6 fusion
  108.4 0.6 dynamic-slice_bitcast_fusion
  109.0 0.7 slice_select_fusion
  109.7 0.7 copy.24
  110.4 0.7 copy.25
  111.1 0.8 copy.26
  111.9 0.7 copy.27
  (5 shorter events, 0.0 us)
Async XLA Ops:
  0.7 0.7 copy-start.7
  0.7 0.7 copy-start.6
  0.7 0.7 copy-start.3
  1.4 0.7 copy-start.4
  1.4 0.7 copy-start.5
  4.2 1.0 copy-start
  4.2 1.0 copy-start.1
  4.2 1.0 copy-start.2
